TPU v7x, 256 devices: a whole 4x4x8 slice. The times are simulated.
256 devices in a mesh: dp: 8 (over y, core), expert: 32 (over z, x).
Axes of the slice: x: 4, y: 4, z: 8, core: 2. Of those that a mesh axis runs over, the one named last changes fastest.
Arguments:
- frames_in: bfloat16 [256, 256, 1024], P(('dp', 'expert')), may hold values from -6 to 6
- pit_order: int32 [128, 2], replicated, may hold values from 0 to 1, each once within a row
- expert_ids: int32 [256, 256, 2], P(('dp', 'expert')), may hold values from 0 to 31, all different within a row; in each aligned block of 256 rows (0 to 255, 256 to 511, ..., all dimensions but the last counted through in order) at most 20 rows name the same one
- norm_gains: float32 [2, 1024], replicated, may hold values from 0.25 to 1.75
- attn_qkv: bfloat16 [3, 1024, 1024], P(None, 'expert'), may hold values from -6 to 6
- attn_out: bfloat16 [1024, 1024], P('expert'), may hold values from -0.1875 to 0.1875
- router: float32 [1024, 32], replicated, may hold values from -0.046875 to 0.046875
- expert_in: bfloat16 [32, 1024, 4096], P('expert', None, 'dp'), may hold values from -0.1875 to 0.1875
- expert_out: bfloat16 [32, 4096, 1024], P('expert', 'dp'), may hold values from -0.09375 to 0.09375
Outputs:
- layer_out: bfloat16 [256, 256, 1024], P(('dp', 'expert'))
Inputs may be any that keep to these rules, and one draw needn't show every extreme that they name: `expert_ids`: at most 20 frames of one stream name the same expert, and in every draw some stream names some expert exactly 20 times; each frame names 2 different experts.
All inputs are finite; a program needn't handle non-finite values.
Results may differ from a plain program's by a relative error of at most 0.011.
Values may be sent and summed in bfloat16 or wider, within the bound.
A program may use at most 128 MiB of HBM per device.

v0:
```python
import jax
import jax.numpy as jnp
from jax import lax
from jax.sharding import PartitionSpec as P

HEAD_DIM = 64
epsilon = 1e-05


def from_partner(block, axis, bit):
    count = lax.axis_size(axis)
    route = []
    for low in range(count):
        high = low | 1 << bit
        if high != low and high < count:
            route += [(low, high), (high, low)]
    return lax.ppermute(block, axis, route)


def layer_norm(values, gain):
    mean = jnp.mean(values, axis=-1, keepdims=True)
    centred = values - mean
    spread = jnp.mean(centred * centred, axis=-1, keepdims=True)
    return centred * lax.rsqrt(spread + epsilon) * gain


def body(
    frames_in, pit_order, expert_ids, norm_gains, attn_qkv, attn_out, router, expert_in, expert_out
):
    dp_count = lax.axis_size("dp")
    exp_count = lax.axis_size("expert")
    dp_index = lax.axis_index("dp")
    exp_index = lax.axis_index("expert")
    frames = frames_in.shape[1]
    width = frames_in.shape[2]
    heads = width // HEAD_DIM
    top = expert_ids.shape[2]
    capacity = frames * top * 5 // (4 * exp_count)
    partner = from_partner(frames_in, "dp", dp_count.bit_length() - 2)
    half = dp_count // 2
    speaker = dp_index // half
    meeting = dp_index % half * exp_count + exp_index
    source = pit_order[meeting, speaker]
    stream = jnp.where(source == speaker, frames_in[0], partner[0])
    resid = stream.astype(jnp.float32)
    normed = layer_norm(resid, norm_gains[0]).astype(jnp.bfloat16)
    columns = normed
    projected = jnp.einsum(
        "fc,jcd->jfd",
        columns,
        lax.all_gather(attn_qkv, "expert", axis=1, tiled=True),
        preferred_element_type=jnp.float32,
    )
    projected = projected.astype(jnp.bfloat16).reshape(3, frames, heads, HEAD_DIM)
    scores = (
        jnp.einsum("qhd,khd->hqk", projected[0], projected[1], preferred_element_type=jnp.float32)
        / HEAD_DIM**0.5
    )
    highest = jnp.max(scores, axis=-1, keepdims=True)
    weights = jnp.exp(scores - highest)
    probs = (weights / jnp.sum(weights, axis=-1, keepdims=True)).astype(jnp.bfloat16)
    context = jnp.einsum("hqk,khd->qhd", probs, projected[2], preferred_element_type=jnp.float32)
    context = context.reshape(frames, width).astype(jnp.bfloat16)
    columns = context
    attended = jnp.dot(
        columns,
        lax.all_gather(attn_out, "expert", axis=0, tiled=True),
        preferred_element_type=jnp.float32,
    )
    mixed = (resid + attended).astype(jnp.bfloat16)
    mixed_wide = mixed.astype(jnp.float32)
    normed2 = layer_norm(mixed_wide, norm_gains[1]).astype(jnp.bfloat16)
    logits = jnp.dot(normed2.astype(jnp.float32), router, precision=lax.Precision.HIGHEST)
    chosen = expert_ids[0]
    picked = jnp.take_along_axis(logits, chosen, axis=1)
    gate_first = jax.nn.sigmoid(picked[:, 0] - picked[:, 1])
    gate_second = 1.0 - gate_first
    flat = chosen.reshape(-1)
    onehot = (flat[:, None] == jnp.arange(exp_count, dtype=jnp.int32)[None, :]).astype(jnp.int32)
    ranks = jnp.sum(onehot * (jnp.cumsum(onehot, axis=0) - 1), axis=1)
    positions = flat * capacity + ranks
    rows = jnp.repeat(normed2, top, axis=0)
    outgoing = jnp.zeros((exp_count * capacity, width), jnp.bfloat16).at[positions].set(rows)
    outgoing = outgoing.reshape(exp_count, capacity, width)
    piece = lax.all_gather(
        lax.all_to_all(outgoing, "expert", split_axis=0, concat_axis=0, tiled=True),
        "dp",
        axis=0,
        tiled=True,
    )
    flat_rows = piece.reshape(-1, piece.shape[-1])
    hidden = jax.nn.silu(
        jnp.dot(flat_rows, expert_in[0], preferred_element_type=jnp.float32)
    ).astype(jnp.bfloat16)
    partials = (
        jnp.dot(hidden, expert_out[0], preferred_element_type=jnp.float32)
        .astype(jnp.bfloat16)
        .reshape(piece.shape)
    )
    summed = lax.psum_scatter(partials, "dp", scatter_dimension=0, tiled=True).astype(jnp.float32)
    answer = summed.astype(jnp.bfloat16)
    returned = lax.all_to_all(answer, "expert", split_axis=0, concat_axis=0, tiled=True)
    back = returned.reshape(exp_count * capacity, width)[positions]
    back = back.reshape(frames, top, width).astype(jnp.float32)
    result = mixed_wide + gate_first[:, None] * back[:, 0] + gate_second[:, None] * back[:, 1]
    return result.astype(jnp.bfloat16)[None]


def solution(mesh):
    return jax.shard_map(
        body,
        mesh=mesh,
        in_specs=(
            P(("dp", "expert"), None, None),
            P(),
            P(("dp", "expert"), None, None),
            P(),
            P(None, "expert", None),
            P("expert", None),
            P(),
            P("expert", None, "dp"),
            P("expert", "dp", None),
        ),
        out_specs=P(("dp", "expert"), None, None),
        check_vma=False,
    )
```

profile of v0, /device:TPU:9, one launch (start us, length us, event | category | flops | bytes accessed | tf_op | source)
XLA Modules:
  0.0 496.9 jit_solution(15275122537670167731)
XLA Ops:
  6.5 0.7 all-gather.4.cloned.1.call-update
  7.3 0.7 all-gather.6.cloned.1.call-update
  8.1 2.1 collective-permute-start
  10.2 0.8 copy.42
  11.3 1.3 dynamic_slice.3
  13.2 0.7 broadcast_multiply_fusion
  14.0 0.1 mul.105
  14.2 1.2 reduce-window.6
  15.4 0.2 slice_reduce_fusion
  15.8 0.8 fusion.57
  16.5 6.1 %collective-permute-done = bf16[1,256,1024]{2,1,0:T(8,128)(2,1)S(1)} collective-permute-done((bf16[1,256,1024]{2,1,0:T(8,128)(2,1)}, bf16[1,256,1024]{2,1,0:T(8,128)(2,1)S(1)}, u32[]{:S(2)}, u32[]{:S(2)}) %collective-permute-start) | collective-permute-done | bytes 524320 | tf_op jit(solution)/shard_map/ppermute | solution.py:17
  22.6 0.2 convert_reduce_fusion.1
  22.9 0.3 fusion.18
  23.2 78.0 %all-gather.4.cloned.1.call-done = bf16[3,1024,1024]{2,1,0:T(8,128)(2,1)} async-done(((bf16[3,32,1024]{2,1,0:T(8,128)(2,1)}), bf16[3,1024,1024]{2,1,0:T(8,128)(2,1)}) %all-gather.4.cloned.1.call-update) | async-done | bytes 6291472 | tf_op jit(solution)/shard_map/all_gather | solution.py:51
  101.1 4.7 fusion.7
  106.0 1.0 copy.40
  107.0 0.2 copy.39
  107.2 0.2 copy.38
  107.4 4.5 fusion.58
  111.9 2.7 fusion.10
  114.6 60.5 %all-gather.6.cloned.1.call-done = bf16[1024,1024]{1,0:T(8,128)(2,1)} async-done(((bf16[32,1024]{1,0:T(8,128)(2,1)}), bf16[1024,1024]{1,0:T(8,128)(2,1)}) %all-gather.6.cloned.1.call-update) | async-done | bytes 2097168 | tf_op jit(solution)/shard_map/all_gather | solution.py:67
  175.1 2.4 convert_reduce_fusion
  177.5 0.3 fusion.15
  177.8 0.5 copy-done.2
  178.3 0.3 fusion.17
  178.6 0.5 broadcast_in_dim.12
  179.1 1.2 reshape.164
  180.4 4.4 scatter_custom_fusion
  184.7 2.2 reshape.141
  187.0 39.2 %all_to_all.10 = bf16[32,20,1024]{2,1,0:T(8,128)(2,1)S(1)} all-to-all(bf16[32,20,1024]{2,1,0:T(8,128)(2,1)S(1)} %reshape.141), channel_id=1, replica_groups=mesh['dp'=8,'expert'=32] {'expert'}, dimensions={0} | all-to-all | bytes 2621440 | tf_op jit(solution)/shard_map/all_to_all | solution.py:86
  226.1 1.8 copy.48
  228.0 63.1 %all-gather.8.cloned.1.call-done = bf16[256,20,1024]{2,0,1:T(8,128)(2,1)} async-done(((bf16[32,20,1024]{2,0,1:T(8,128)(2,1)}), bf16[256,20,1024]{2,0,1:T(8,128)(2,1)}) %all-gather.8.cloned.1.call-update) | async-done | bytes 10485776 | tf_op jit(solution)/shard_map/all_gather | solution.py:85
  291.1 14.1 %copy.49 = bf16[256,20,1024]{2,1,0:T(8,128)(2,1)} copy(bf16[256,20,1024]{2,0,1:T(8,128)(2,1)} %all-gather.8.cloned.1.call-done) | data formatting | bytes 20971520 | tf_op jit(solution)/shard_map/all_gather | solution.py:85
  305.2 16.5 %reshape.142 = bf16[5120,1024]{1,0:T(8,128)(2,1)} reshape(bf16[256,20,1024]{2,1,0:T(8,128)(2,1)} %copy.49) | data formatting | bytes 20971520 | tf_op jit(solution)/shard_map/reshape | solution.py:91
  321.8 17.1 %convolution_convert_fusion = bf16[5120,1024]{1,0:T(8,128)(2,1)} fusion(bf16[1,512,1024]{2,1,0:T(8,128)(2,1)S(1)} %copy-done, bf16[5120,1024]{1,0:T(8,128)(2,1)} %reshape.142, bf16[1,1024,512]{2,1,0:T(8,128)(2,1)S(1)} %copy-done.6), kind=kOutput, calls=%fused_computation.5 | convolution fusion | flops 10755768320 | bytes 23068672 | tf_op jit(solution)/shard_map/dot_general | solution.py:96
  338.8 16.3 %reshape.143 = bf16[256,20,1024]{2,1,0:T(8,128)(2,1)} reshape(bf16[5120,1024]{1,0:T(8,128)(2,1)} %convolution_convert_fusion) | data formatting | bytes 20971520 | tf_op jit(solution)/shard_map/reshape | solution.py:98
  355.2 74.8 %reduce-scatter.2.cloned.1.call-done = bf16[32,20,1024]{2,1,0:T(8,128)(2,1)} async-done(((bf16[256,20,1024]{2,1,0:T(8,128)(2,1)}), bf16[32,20,1024]{2,1,0:T(8,128)(2,1)}) %reduce-scatter.2.cloned.1.call-update) | async-done | bytes 1310736 | tf_op jit(solution)/shard_map/reduce_scatter | solution.py:100
  430.0 9.9 %all-to-all-start.1 = ((bf16[32,20,1024]{2,1,0:T(8,128)(2,1)}), bf16[32,20,1024]{2,1,0:T(8,128)(2,1)}, u32[]{:S(2)}, u32[]{:S(2)}) async-start(bf16[32,20,1024]{2,1,0:T(8,128)(2,1)} %reduce-scatter.2.cloned.1.call-done), calls=%async_computation.2 | async-start | bytes 3145728 | tf_op jit(solution)/shard_map/all_to_all | solution.py:102
  440.1 0.1 reshape.154
  440.3 0.6 fusion.59
  440.8 4.5 gather_fusion.1
  445.6 0.2 fusion.54
  445.8 34.2 %all-to-all-done.1 = bf16[32,20,1024]{2,1,0:T(8,128)(2,1)} async-done(((bf16[32,20,1024]{2,1,0:T(8,128)(2,1)}), bf16[32,20,1024]{2,1,0:T(8,128)(2,1)}, u32[]{:S(2)}, u32[]{:S(2)}) %all-to-all-start.1) | async-done | bytes 1310752 | tf_op jit(solution)/shard_map/all_to_all | solution.py:102
  480.0 2.3 reshape.144
  482.2 2.8 gather_fusion
  485.0 2.5 reshape.145
  487.5 1.6 fusion.55
  489.2 1.2 fusion.34
  (37 shorter events, 1.2 us)
Async XLA Ops:
  6.5 315.2 %copy-start = (bf16[1,512,1024]{2,1,0:T(8,128)(2,1)S(1)}, bf16[1,512,1024]{2,1,0:T(8,128)(2,1)}, u32[]{:S(2)}) copy-start(bf16[1,512,1024]{2,1,0:T(8,128)(2,1)} %param.17) | copy-start | bytes 3145732
  6.5 94.6 %all-gather.4.cloned.1.call-start = ((), (), s32[]{:S(2)}) async-start(), calls=%async_computation.3 | async-start | bytes 6488064 | tf_op jit(solution)/shard_map/all_gather | solution.py:51
  7.3 167.8 %all-gather.6.cloned.1.call-start = ((), (), s32[]{:S(2)}) async-start(), calls=%async_computation.4 | async-start | bytes 2162688 | tf_op jit(solution)/shard_map/all_gather | solution.py:67
  8.0 283.1 %all-gather.8.cloned.1.call-start = ((), (), s32[]{:S(2)}) async-start(), calls=%async_computation.5 | async-start | bytes 11796480 | tf_op jit(solution)/shard_map/all_gather | solution.py:85
  8.1 14.6 %collective-permute-start = (bf16[1,256,1024]{2,1,0:T(8,128)(2,1)}, bf16[1,256,1024]{2,1,0:T(8,128)(2,1)S(1)}, u32[]{:S(2)}, u32[]{:S(2)}) collective-permute-start(bf16[1,256,1024]{2,1,0:T(8,128)(2,1)} %param.9), channel_id=1, source_target_pairs={{0,128},{128,0},{32,160},{160,32},{64,192},{192,64},{96,224},{224,... | collective-permute-start | bytes 1572872 | tf_op jit(solution)/shard_map/ppermute | solution.py:17
  177.5 0.8 copy-start.2
  227.9 202.1 %reduce-scatter.2.cloned.1.call-start = ((), (), s32[]{:S(2)}) async-start(), calls=%async_computation.6 | async-start | bytes 14155776 | tf_op jit(solution)/shard_map/reduce_scatter | solution.py:100
  305.2 16.5 %copy-start.6 = (bf16[1,1024,512]{2,1,0:T(8,128)(2,1)S(1)}, bf16[1,1024,512]{2,1,0:T(8,128)(2,1)}, u32[]{:S(2)}) copy-start(bf16[1,1024,512]{2,1,0:T(8,128)(2,1)} %param.16) | copy-start | bytes 3145732
  355.2 84.7 %copy-start.5 = (s32[1,256,2]{1,2,0:T(2,128)S(1)}, s32[1,256,2]{1,2,0:T(2,128)}, u32[]{:S(2)}) copy-start(s32[1,256,2]{1,2,0:T(2,128)} %param.11) | copy-start | bytes 6148
  355.2 85.0 %copy-start.4 = (f32[1024,32]{0,1:T(8,128)S(1)}, f32[1024,32]{0,1:T(8,128)}, u32[]{:S(2)}) copy-start(f32[1024,32]{0,1:T(8,128)} %param.15) | copy-start | bytes 393220
  430.0 49.9 %all-to-all-start.1 = ((bf16[32,20,1024]{2,1,0:T(8,128)(2,1)}), bf16[32,20,1024]{2,1,0:T(8,128)(2,1)}, u32[]{:S(2)}, u32[]{:S(2)}) async-start(bf16[32,20,1024]{2,1,0:T(8,128)(2,1)} %reduce-scatter.2.cloned.1.call-done), calls=%async_computation.2 | async-start | bytes 3145728 | tf_op jit(solution)/shard_map/all_to_all | solution.py:102
  485.0 5.4 %copy-start.1 = (bf16[1,512,1024]{2,1,0:T(8,128)(2,1)S(1)}, bf16[1,512,1024]{2,1,0:T(8,128)(2,1)}, u32[]{:S(2)}) copy-start(bf16[1,512,1024]{2,1,0:T(8,128)(2,1)} %param.17) | copy-start | bytes 3145732
  487.5 1.6 copy-start.3
Sparse Core Ops, SparseCore 0:
  9.9 91.1 all-gather.3
  103.7 71.3 all-gather.5
  228.1 62.9 all-gather.7
  355.3 74.6 reduce-scatter.1
where the time goes:
time: 499 us; the launch traced here: 497 us
  waiting for transfers between devices  318 us (64%)
  local copies, waits for them, and re-layouts  76.9 us (15%)
  blocking collectives  39.2 us (8%)
  matrix products  31.9 us (6%)
  between operations  14.1 us (3%)
  starting transfers between devices  12.1 us (2%)
    all_gather x1, waiting for transfers between devices, body(): lax.all_gather(attn_qkv, 'expert', axis=1, tiled=True)  78 us
    reduce_scatter x1, waiting for transfers between devices, body(): lax.psum_scatter(partials, 'dp', scatter_dimension=0, tiled=True)  74.8 us
    all_gather x1, waiting for transfers between devices, body(): lax.all_gather(lax.all_to_all(outgoing, 'expert', split_axis=0, concat_ax...  63.1 us
    all_gather x1, waiting for transfers between devices, body(): lax.all_gather(attn_out, 'expert', axis=0, tiled=True)  60.5 us
    all_to_all x1, blocking collectives, body(): lax.all_to_all(outgoing, 'expert', split_axis=0, concat_axis=0, tiled=True)  39.2 us
    all_to_all x1, waiting for transfers between devices, body(): lax.all_to_all(answer, 'expert', split_axis=0, concat_axis=0, tiled=True)  34.2 us
    dot_general x1, matrix products, body(): jnp.dot(hidden, expert_out[0], preferred_element_type=jnp.float32)  17.1 us
    reshape x1, local copies, waits for them, and re-layouts, body(): flat_rows = piece.reshape(-1, piece.shape[-1])  16.5 us
  transfers between devices with their start and end apart: 6, of which 6 were waited for; matrix products, arithmetic and copies ran while one was open for 5% of the time, Pallas kernels for 0%

commit v1 on v0

--- a/solution.py
+++ b/solution.py
@@ -48,7 +48,9 @@
     projected = jnp.einsum(
         "fc,jcd->jfd",
         columns,
-        lax.all_gather(attn_qkv, "expert", axis=1, tiled=True),
+        jnp.concatenate(
+            lax.all_to_all(jnp.stack([attn_qkv] * lax.axis_size("expert")), "expert", 0, 0), axis=1
+        ),
         preferred_element_type=jnp.float32,
     )
     projected = projected.astype(jnp.bfloat16).reshape(3, frames, heads, HEAD_DIM)

time: 499 us -> 517 us (1.036)
  starting transfers between devices: 12.1 us -> 23.4 us
  blocking collectives: 39.2 us -> 50.5 us
  waiting for transfers between devices: 318 us -> 312 us
  local copies, waits for them, and re-layouts: 76.9 us -> 82.8 us
    all_to_all x0 -> x1, waiting for transfers between devices: none -> 134 us  [body(): lax.all_to_all(jnp.stack([attn_qkv] * lax.axis_size('expert')), 'expert',...]
    all_gather x1 -> x0, waiting for transfers between devices: 78 us -> none  [body(): lax.all_gather(attn_qkv, 'expert', axis=1, tiled=True)]
    all_gather x1, waiting for transfers between devices: 60.5 us -> 0.02 us  [body(): lax.all_gather(attn_out, 'expert', axis=0, tiled=True)]
    all_to_all x1, blocking collectives: 39.2 us -> 50.5 us  [body(): lax.all_to_all(outgoing, 'expert', split_axis=0, concat_axis=0, tiled=True)]
    all_to_all x0 -> x1, starting transfers between devices: none -> 11.3 us  [body(): lax.all_to_all(jnp.stack([attn_qkv] * lax.axis_size('expert')), 'expert',...]
  transfers between devices with their start and end apart: 6 -> 6, of which waited for: 6 -> 5; matrix products, arithmetic and copies ran while one was open for 5% -> 5% of each run, Pallas kernels for 0% -> 0%
where the time goes in v1:
time: 517 us; the launch traced here: 515 us
  waiting for transfers between devices  312 us (60%)
  local copies, waits for them, and re-layouts  82.8 us (16%)
  blocking collectives  50.5 us (10%)
  matrix products  29.2 us (6%)
  starting transfers between devices  23.4 us (5%)
  between operations  14.1 us (3%)
    all_to_all x1, waiting for transfers between devices, body(): lax.all_to_all(jnp.stack([attn_qkv] * lax.axis_size('expert')), 'expert',...  134 us
    reduce_scatter x1, waiting for transfers between devices, body(): lax.psum_scatter(partials, 'dp', scatter_dimension=0, tiled=True)  74.8 us
    all_gather x1, waiting for transfers between devices, body(): lax.all_gather(lax.all_to_all(outgoing, 'expert', split_axis=0, concat_ax...  59.6 us
    all_to_all x1, blocking collectives, body(): lax.all_to_all(outgoing, 'expert', split_axis=0, concat_axis=0, tiled=True)  50.5 us
    all_to_all x1, waiting for transfers between devices, body(): lax.all_to_all(answer, 'expert', split_axis=0, concat_axis=0, tiled=True)  34.2 us
    dot_general x1, matrix products, body(): jnp.dot(hidden, expert_out[0], preferred_element_type=jnp.float32)  17.1 us
    reshape x1, local copies, waits for them, and re-layouts, body(): flat_rows = piece.reshape(-1, piece.shape[-1])  16.5 us
    reshape x1, local copies, waits for them, and re-layouts, body(): partials = jnp.dot(hidden, expert_out[0], preferred_element_type=jnp.floa...  16.3 us
  transfers between devices with their start and end apart: 6, of which 5 were waited for; matrix products, arithmetic and copies ran while one was open for 5% of the time, Pallas kernels for 0%

profile of v1, /device:TPU:9, one launch (start us, length us, event | category | flops | bytes accessed | tf_op | source)
XLA Modules:
  0.0 515.4 jit_solution(17259195047188140655)
XLA Ops:
  6.5 4.5 stack.2
  11.0 11.3 %all-to-all-start = ((bf16[32,3,32,1024]{3,2,1,0:T(8,128)(2,1)}), bf16[32,3,32,1024]{3,2,1,0:T(8,128)(2,1)}, u32[]{:S(2)}, u32[]{:S(2)}) async-start(bf16[32,3,32,1024]{3,2,1,0:T(8,128)(2,1)} %stack.2), calls=%async_computation | async-start | bytes 12582912 | tf_op jit(solution)/shard_map/all_to_all | solution.py:52
  22.4 0.7 all-gather.3.cloned.1.call-update
  23.1 2.1 collective-permute-start
  25.4 0.1 eq.35
  25.5 0.1 eq.31
  25.7 0.6 dynamic_slice.3
  27.1 0.1 mul.107
  27.2 1.2 reduce-window.6
  28.4 0.2 slice_reduce_fusion
  28.8 8.5 %collective-permute-done = bf16[1,256,1024]{2,1,0:T(8,128)(2,1)S(1)} collective-permute-done((bf16[1,256,1024]{2,1,0:T(8,128)(2,1)S(1)}, bf16[1,256,1024]{2,1,0:T(8,128)(2,1)S(1)}, u32[]{:S(2)}, u32[]{:S(2)}) %collective-permute-start) | collective-permute-done | bytes 524320 | tf_op jit(solution)/shard_map/ppermute | solution.py:17
  37.3 0.2 convert_reduce_fusion.1
  37.5 0.3 fusion.17
  37.8 133.7 %all-to-all-done = bf16[32,3,32,1024]{3,2,1,0:T(8,128)(2,1)} async-done(((bf16[32,3,32,1024]{3,2,1,0:T(8,128)(2,1)}), bf16[32,3,32,1024]{3,2,1,0:T(8,128)(2,1)}, u32[]{:S(2)}, u32[]{:S(2)}) %all-to-all-start) | async-done | bytes 6291488 | tf_op jit(solution)/shard_map/all_to_all | solution.py:52
  171.5 3.5 copy.38
  175.0 1.9 fusion.7
  177.1 1.0 copy.41
  178.1 0.2 copy.40
  178.3 0.2 copy.39
  178.5 4.5 fusion.58
  183.0 2.7 fusion.10
  185.7 2.4 convert_reduce_fusion
  188.2 0.3 fusion.13
  188.5 0.5 copy-done.2
  188.9 0.3 fusion.15
  189.2 0.5 broadcast_in_dim.12
  189.8 1.2 reshape.195
  191.0 4.4 scatter_custom_fusion
  195.4 2.2 reshape.172
  197.6 50.5 %all_to_all.15 = bf16[32,20,1024]{2,1,0:T(8,128)(2,1)S(1)} all-to-all(bf16[32,20,1024]{2,1,0:T(8,128)(2,1)S(1)} %reshape.172), channel_id=1, replica_groups=mesh['dp'=8,'expert'=32] {'expert'}, dimensions={0} | all-to-all | bytes 2621440 | tf_op jit(solution)/shard_map/all_to_all | solution.py:88
  248.1 1.8 copy.49
  250.0 59.6 %all-gather.5.cloned.1.call-done = bf16[256,20,1024]{2,0,1:T(8,128)(2,1)} async-done(((bf16[32,20,1024]{2,0,1:T(8,128)(2,1)}), bf16[256,20,1024]{2,0,1:T(8,128)(2,1)}) %all-gather.5.cloned.1.call-update) | async-done | bytes 10485776 | tf_op jit(solution)/shard_map/all_gather | solution.py:87
  309.6 14.1 %copy.50 = bf16[256,20,1024]{2,1,0:T(8,128)(2,1)} copy(bf16[256,20,1024]{2,0,1:T(8,128)(2,1)} %all-gather.5.cloned.1.call-done) | data formatting | bytes 20971520 | tf_op jit(solution)/shard_map/all_gather | solution.py:87
  323.7 16.5 %reshape.173 = bf16[5120,1024]{1,0:T(8,128)(2,1)} reshape(bf16[256,20,1024]{2,1,0:T(8,128)(2,1)} %copy.50) | data formatting | bytes 20971520 | tf_op jit(solution)/shard_map/reshape | solution.py:93
  340.3 17.1 %convolution_convert_fusion = bf16[5120,1024]{1,0:T(8,128)(2,1)} fusion(bf16[1,512,1024]{2,1,0:T(8,128)(2,1)S(1)} %copy-done, bf16[5120,1024]{1,0:T(8,128)(2,1)} %reshape.173, bf16[1,1024,512]{2,1,0:T(8,128)(2,1)S(1)} %copy-done.9), kind=kOutput, calls=%fused_computation.5 | convolution fusion | flops 10755768320 | bytes 23068672 | tf_op jit(solution)/shard_map/dot_general | solution.py:98
  357.4 16.3 %reshape.174 = bf16[256,20,1024]{2,1,0:T(8,128)(2,1)} reshape(bf16[5120,1024]{1,0:T(8,128)(2,1)} %convolution_convert_fusion) | data formatting | bytes 20971520 | tf_op jit(solution)/shard_map/reshape | solution.py:100
  373.7 74.8 %reduce-scatter.2.cloned.1.call-done = bf16[32,20,1024]{2,1,0:T(8,128)(2,1)} async-done(((bf16[256,20,1024]{2,1,0:T(8,128)(2,1)}), bf16[32,20,1024]{2,1,0:T(8,128)(2,1)}) %reduce-scatter.2.cloned.1.call-update) | async-done | bytes 1310736 | tf_op jit(solution)/shard_map/reduce_scatter | solution.py:102
  448.6 9.9 %all-to-all-start.2 = ((bf16[32,20,1024]{2,1,0:T(8,128)(2,1)}), bf16[32,20,1024]{2,1,0:T(8,128)(2,1)}, u32[]{:S(2)}, u32[]{:S(2)}) async-start(bf16[32,20,1024]{2,1,0:T(8,128)(2,1)} %reduce-scatter.2.cloned.1.call-done), calls=%async_computation.3 | async-start | bytes 3145728 | tf_op jit(solution)/shard_map/all_to_all | solution.py:104
  458.6 0.1 reshape.185
  458.8 0.6 fusion.59
  459.3 4.5 gather_fusion.1
  464.1 0.2 fusion.54
  464.3 34.2 %all-to-all-done.2 = bf16[32,20,1024]{2,1,0:T(8,128)(2,1)} async-done(((bf16[32,20,1024]{2,1,0:T(8,128)(2,1)}), bf16[32,20,1024]{2,1,0:T(8,128)(2,1)}, u32[]{:S(2)}, u32[]{:S(2)}) %all-to-all-start.2) | async-done | bytes 1310752 | tf_op jit(solution)/shard_map/all_to_all | solution.py:104
  498.5 2.3 reshape.175
  500.7 2.8 gather_fusion
  503.5 2.5 reshape.176
  506.0 1.6 fusion.55
  507.7 1.2 fusion.34
  (44 shorter events, 1.1 us)
Async XLA Ops:
  6.5 333.7 %copy-start = (bf16[1,512,1024]{2,1,0:T(8,128)(2,1)S(1)}, bf16[1,512,1024]{2,1,0:T(8,128)(2,1)}, u32[]{:S(2)}) copy-start(bf16[1,512,1024]{2,1,0:T(8,128)(2,1)} %param.17) | copy-start | bytes 3145732
  11.0 12.1 %copy-start.4 = (bf16[1,256,1024]{2,1,0:T(8,128)(2,1)S(1)}, bf16[1,256,1024]{2,1,0:T(8,128)(2,1)}, u32[]{:S(2)}) copy-start(bf16[1,256,1024]{2,1,0:T(8,128)(2,1)} %param.9) | copy-start | bytes 1572868
  11.0 14.2 %copy-start.6 = (s32[1,256,2]{1,2,0:T(2,128)S(1)}, s32[1,256,2]{1,2,0:T(2,128)}, u32[]{:S(2)}) copy-start(s32[1,256,2]{1,2,0:T(2,128)} %param.11) | copy-start | bytes 6148
  11.0 14.7 %copy-start.8 = (s32[128,2]{0,1:T(2,128)S(1)}, s32[128,2]{0,1:T(2,128)}, u32[]{:S(2)}) copy-start(s32[128,2]{0,1:T(2,128)} %param.10) | copy-start | bytes 3076
  11.0 17.8 %copy-start.7 = (f32[2,1024]{1,0:T(2,128)S(1)}, f32[2,1024]{1,0:T(2,128)}, u32[]{:S(2)}) copy-start(f32[2,1024]{1,0:T(2,128)} %param.12) | copy-start | bytes 24580
  11.0 160.5 %all-to-all-start = ((bf16[32,3,32,1024]{3,2,1,0:T(8,128)(2,1)}), bf16[32,3,32,1024]{3,2,1,0:T(8,128)(2,1)}, u32[]{:S(2)}, u32[]{:S(2)}) async-start(bf16[32,3,32,1024]{3,2,1,0:T(8,128)(2,1)} %stack.2), calls=%async_computation | async-start | bytes 12582912 | tf_op jit(solution)/shard_map/all_to_all | solution.py:52
  22.3 163.4 %all-gather.3.cloned.1.call-start = ((), (), s32[]{:S(2)}) async-start(), calls=%async_computation.4 | async-start | bytes 2162688 | tf_op jit(solution)/shard_map/all_gather | solution.py:69
  23.1 286.6 %all-gather.5.cloned.1.call-start = ((), (), s32[]{:S(2)}) async-start(), calls=%async_computation.5 | async-start | bytes 11796480 | tf_op jit(solution)/shard_map/all_gather | solution.py:87
  23.1 14.2 %collective-permute-start = (bf16[1,256,1024]{2,1,0:T(8,128)(2,1)S(1)}, bf16[1,256,1024]{2,1,0:T(8,128)(2,1)S(1)}, u32[]{:S(2)}, u32[]{:S(2)}) collective-permute-start(bf16[1,256,1024]{2,1,0:T(8,128)(2,1)S(1)} %copy-done.4), channel_id=1, source_target_pairs={{0,128},{128,0},{32,160},{160,32},{64,192},{192,64},{96,224},{224,... | collective-permute-start | bytes 1572872 | tf_op jit(solution)/shard_map/ppermute | solution.py:17
  188.1 0.8 copy-start.2
  249.9 198.6 %reduce-scatter.2.cloned.1.call-start = ((), (), s32[]{:S(2)}) async-start(), calls=%async_computation.6 | async-start | bytes 14155776 | tf_op jit(solution)/shard_map/reduce_scatter | solution.py:102
  323.7 16.5 %copy-start.9 = (bf16[1,1024,512]{2,1,0:T(8,128)(2,1)S(1)}, bf16[1,1024,512]{2,1,0:T(8,128)(2,1)}, u32[]{:S(2)}) copy-start(bf16[1,1024,512]{2,1,0:T(8,128)(2,1)} %param.16) | copy-start | bytes 3145732
  373.7 85.0 %copy-start.5 = (f32[1024,32]{0,1:T(8,128)S(1)}, f32[1024,32]{0,1:T(8,128)}, u32[]{:S(2)}) copy-start(f32[1024,32]{0,1:T(8,128)} %param.15) | copy-start | bytes 393220
  448.6 49.9 %all-to-all-start.2 = ((bf16[32,20,1024]{2,1,0:T(8,128)(2,1)}), bf16[32,20,1024]{2,1,0:T(8,128)(2,1)}, u32[]{:S(2)}, u32[]{:S(2)}) async-start(bf16[32,20,1024]{2,1,0:T(8,128)(2,1)} %reduce-scatter.2.cloned.1.call-done), calls=%async_computation.3 | async-start | bytes 3145728 | tf_op jit(solution)/shard_map/all_to_all | solution.py:104
  503.5 5.4 %copy-start.1 = (bf16[1,512,1024]{2,1,0:T(8,128)(2,1)S(1)}, bf16[1,512,1024]{2,1,0:T(8,128)(2,1)}, u32[]{:S(2)}) copy-start(bf16[1,512,1024]{2,1,0:T(8,128)(2,1)} %param.17) | copy-start | bytes 3145732
  506.0 1.6 copy-start.3
Sparse Core Ops, SparseCore 0:
  25.7 117.8 all-gather.2
  250.0 59.5 all-gather.4
  373.9 74.6 reduce-scatter.1
